TPU v7x, 256 devices: a whole 4x4x8 slice. The times are simulated.
256 devices in a mesh: dp: 4 (over z_lo, core), seq: 64 (over z_hi, y, x).
Axes of the slice: x: 4, y: 4, z: 8 (z_hi: 4, z_lo: 2; z = z_hi * 2 + z_lo), core: 2. Of those that a mesh axis runs over, the one named last changes fastest.
Arguments:
- glu_out: bfloat16 [4, 8192, 1536], P('dp', 'seq'), may hold values from -6 to 6
- lengths: int32 [4], replicated, may hold values from 1024 to 8192, as said below
- kernel: float32 [31, 1536], replicated, may hold values from -1 to 1
- gain: float32 [1536], replicated, may hold values from 0.25 to 1.75
- bias: float32 [1536], replicated, may hold values from -3 to 3
- weight: bfloat16 [1536, 1536], P(('dp', 'seq')), may hold values from -0.15625 to 0.15625
- master: float32 [1536, 1536], P(('dp', 'seq')), may hold values from -0.15625 to 0.15625
- moment_one: float32 [1536, 1536], P(('dp', 'seq')), may hold values from -120 to 120
- moment_two: float32 [1536, 1536], P(('dp', 'seq')), may hold values from 100 to 100000
- cotangent: bfloat16 [4, 8192, 1536], P('dp', 'seq'), may hold values from -6 to 6
Outputs:
- module_out: bfloat16 [4, 8192, 1536], P('dp', 'seq')
- input_grad: bfloat16 [4, 8192, 1536], P('dp', 'seq')
- kernel_grad: float32 [31, 1536], replicated
- gain_grad: float32 [1536], replicated
- bias_grad: float32 [1536], replicated
- new_master: float32 [1536, 1536], P(('dp', 'seq'))
- new_one: float32 [1536, 1536], P(('dp', 'seq'))
- new_two: float32 [1536, 1536], P(('dp', 'seq'))
Inputs may be any that keep to these rules, and one draw needn't show every extreme that they name: `lengths`: in every draw one stream has all 8192 frames valid; each other stream has between 1024 and 2730 valid frames.
All inputs are finite; a program needn't handle non-finite values.
Results may differ from a plain program's by a relative error of at most 0.0049.
Values may be sent and summed in bfloat16 or wider, within the bound.
No kernel may reach another device: no remote copies, remote signals or barrier semaphores. Data moves between devices by JAX's collectives and lax.ppermute only.
A program may use at most 64 MiB of HBM per device.

v0:
```python
import jax
import jax.numpy as jnp
from jax import lax
from jax.sharding import PartitionSpec as P

KERNEL = 31
HALF = 15
beta_one = 0.9
beta_two = 0.999
adam_rate = 0.001
adam_eps = 1e-08
norm_eps = 1e-05
first_fix = 0.9999734386011124
second_fix = 0.09520785288629043


def with_halo(block, sides, width):
    for axis, dim in sides:
        count = lax.axis_size(axis)
        forward = [(i, i + 1) for i in range(count - 1)]
        backward = [(target, source) for source, target in forward]
        low = lax.ppermute(
            lax.slice_in_dim(block, block.shape[dim] - width, None, axis=dim), axis, forward
        )
        high = lax.ppermute(lax.slice_in_dim(block, 0, width, axis=dim), axis, backward)
        block = jnp.concatenate([low, block, high], axis=dim)
    return block


def on_device(
    glu_out, lengths, kernel, gain, bias, weight, master, moment_one, moment_two, cotangent
):
    frames = glu_out.shape[1]
    stream = lax.axis_index("dp")
    shard = lax.axis_index("seq")
    positions = shard * frames + jnp.arange(frames, dtype=jnp.int32)
    valid = (positions < lengths[stream])[:, None]
    count = jnp.sum(lengths).astype(jnp.float32)
    masked = jnp.where(valid, glu_out[0], jnp.zeros((), glu_out.dtype))
    padded = with_halo(masked, (("seq", 0),), HALF).astype(jnp.float32)
    conv_out = jnp.zeros((frames, masked.shape[1]), jnp.float32)
    for tap in range(KERNEL):
        conv_out = conv_out + kernel[tap] * padded[tap : tap + frames]
    total = lax.psum(jnp.sum(jnp.where(valid, conv_out, 0.0), axis=0), ("dp", "seq"))
    channel_mean = total / count
    deviation = jnp.where(valid, conv_out - channel_mean, 0.0)
    spread = lax.psum(jnp.sum(deviation * deviation, axis=0), ("dp", "seq"))
    channel_var = spread / count
    inv_std = lax.rsqrt(channel_var + norm_eps)
    standard = (conv_out - channel_mean) * inv_std
    scaled = gain * standard + bias
    logistic = jax.nn.sigmoid(scaled)
    hidden = (scaled * logistic).astype(jnp.bfloat16)
    grad_out = jnp.where(valid, cotangent[0], jnp.zeros((), cotangent.dtype))
    columns = hidden
    product = jnp.dot(
        columns,
        lax.all_gather(weight, ("dp", "seq"), axis=0, tiled=True),
        preferred_element_type=jnp.float32,
    )
    hidden_grad = lax.dot_general(
        grad_out,
        lax.all_gather(weight, ("dp", "seq"), axis=0, tiled=True),
        (((1,), (1,)), ((), ())),
        preferred_element_type=jnp.float32,
    )
    module_out = jnp.where(valid, product, 0.0).astype(jnp.bfloat16)
    scaled_grad = hidden_grad * logistic * (1.0 + scaled * (1.0 - logistic))
    gain_grad, bias_grad = lax.psum(
        (jnp.sum(scaled_grad * standard, axis=0), jnp.sum(scaled_grad, axis=0)), ("dp", "seq")
    )
    conv_grad = jnp.where(
        valid,
        inv_std
        * (gain * scaled_grad - gain * bias_grad / count - standard * gain * gain_grad / count),
        0.0,
    )
    grad_pad = with_halo(conv_grad, (("seq", 0),), HALF)
    flipped = jnp.zeros((frames, conv_grad.shape[1]), jnp.float32)
    for tap in range(KERNEL):
        flipped = flipped + kernel[tap] * grad_pad[2 * HALF - tap : 2 * HALF - tap + frames]
    input_grad = jnp.where(valid, flipped, 0.0).astype(jnp.bfloat16)
    tap_rows = []
    for tap in range(KERNEL):
        tap_rows.append(jnp.sum(conv_grad * padded[tap : tap + frames], axis=0))
    kernel_grad = lax.psum(jnp.stack(tap_rows), ("dp", "seq"))
    columns = hidden
    weight_grad = lax.psum_scatter(
        lax.dot_general(
            columns, grad_out, (((0,), (0,)), ((), ())), preferred_element_type=jnp.float32
        ),
        ("dp", "seq"),
        scatter_dimension=0,
        tiled=True,
    )
    new_one = beta_one * moment_one + (1.0 - beta_one) * weight_grad
    new_two = beta_two * moment_two + (1.0 - beta_two) * weight_grad * weight_grad
    new_master = master - adam_rate * (new_one / first_fix) / (
        jnp.sqrt(new_two / second_fix) + adam_eps
    )
    return (
        module_out[None],
        input_grad[None],
        kernel_grad,
        gain_grad,
        bias_grad,
        new_master,
        new_one,
        new_two,
    )


def solution(mesh):
    return jax.shard_map(
        on_device,
        mesh=mesh,
        in_specs=(
            P("dp", "seq", None),
            P(),
            P(),
            P(),
            P(),
            P(("dp", "seq"), None),
            P(("dp", "seq"), None),
            P(("dp", "seq"), None),
            P(("dp", "seq"), None),
            P("dp", "seq", None),
        ),
        out_specs=(
            P("dp", "seq", None),
            P("dp", "seq", None),
            P(),
            P(),
            P(),
            P(("dp", "seq"), None),
            P(("dp", "seq"), None),
            P(("dp", "seq"), None),
        ),
        check_vma=False,
    )
```

profile of v0, /device:TPU:1, one launch (start us, length us, event | category | flops | bytes accessed | tf_op | source)
XLA Modules:
  0.0 2008.2 jit_solution(8663492157685845760)
XLA Ops:
  25.6 85.3 %psum.35 = f32[1536]{0:T(1024)S(1)} all-reduce(f32[1536]{0:T(1024)S(1)} %get-tuple-element.78), channel_id=1, replica_groups=mesh['dp'=4,'seq'=64] {'dp','seq'}, use_global_device_ids=true, to_apply=%region_1.2 | all-reduce | flops 1536 | bytes 12288 | tf_op jit(solution)/shard_map/psum | solution.py:44
  111.1 73.7 %psum.36 = f32[1536]{0:T(1024)S(1)} all-reduce(f32[1536]{0:T(1024)S(1)} %multiply_reduce_fusion.32), channel_id=1, replica_groups=mesh['dp'=4,'seq'=64] {'dp','seq'}, use_global_device_ids=true, to_apply=%region_4.5 | all-reduce | flops 1536 | bytes 12288 | tf_op jit(solution)/shard_map/psum | solution.py:47
  190.0 808.0 %fusion = f32[8,1536]{1,0:T(8,128)S(1)} fusion(f32[1536,1536]{1,0:T(8,128)} %fusion.95), kind=kCustom, calls=%all-reduce-scatter | all-reduce-scatter fusion | flops 3145729 | bytes 9486336
  998.0 48.1 %collective-permute-start.66 = (f32[8,1536]{1,0:T(8,128)S(1)}, f32[8,1536]{1,0:T(8,128)S(1)}, u32[]{:S(2)}, u32[]{:S(2)}) collective-permute-start(f32[8,1536]{1,0:T(8,128)S(1)} %fusion), channel_id=1, source_target_pairs={{0,63},{1,64},{2,65},{3,66},{4,67},{5,68},{6,69},{7,70},{8,71},{9,... | collective-permute-start | bytes 147464
  1132.1 15.0 collective-permute-start.34
  1147.1 13.1 collective-permute-start.33
  1160.3 13.1 collective-permute-start.32
  1173.4 13.1 collective-permute-start.31
  1186.6 13.1 collective-permute-start.30
  1199.7 13.1 collective-permute-start.29
  1212.9 13.1 collective-permute-start.28
  1226.0 13.1 collective-permute-start.27
  1239.2 13.1 collective-permute-start.26
  1252.3 13.1 collective-permute-start.25
  1265.5 13.1 collective-permute-start.24
  1278.6 13.1 collective-permute-start.23
  1291.8 13.1 collective-permute-start.22
  1304.9 13.1 collective-permute-start.21
  1318.1 13.1 collective-permute-start.20
  1331.2 13.1 collective-permute-start.19
  1344.4 13.1 collective-permute-start.18
  1357.5 13.1 collective-permute-start.17
  1370.7 13.1 collective-permute-start.16
  1383.8 13.1 collective-permute-start.15
  1475.9 13.1 collective-permute-start.8
  1489.0 13.1 collective-permute-start.7
  1502.2 13.1 collective-permute-start.6
  1515.3 13.1 collective-permute-start.5
  1528.5 13.3 collective-permute-start.4
  1554.2 97.0 %concatenate.41 = f32[518,1536]{1,0:T(8,128)} concatenate(f32[6,1536]{1,0:T(8,128)S(1)} %collective-permute-done.67, f32[8,1536]{1,0:T(8,128)S(1)} %collective-permute-done.66, f32[8,1536]{1,0:T(8,128)S(1)} %collective-permute-done.65, f32[8,1536]{1,0:T(8,128)S(1)} %collective-permute-done.64, f32[8,1536]{1,0:T(8,128)S(1)} %collective-permute-done.63, ...), dimensions={0} | concatenate | bytes 6365184
  1665.4 72.6 %all-reduce.2 = (f32[1536]{0:T(1024)}, f32[1536]{0:T(1024)S(1)}) all-reduce(f32[1536]{0:T(1024)S(1)} %get-tuple-element.40, f32[1536]{0:T(1024)S(1)} %get-tuple-element.39), channel_id=1, replica_groups=mesh['dp'=4,'seq'=64] {'dp','seq'}, use_global_device_ids=true, to_apply=%region_8.9 | all-reduce | flops 3072 | bytes 24576 | tf_op jit(solution)/shard_map/psum | solution.py:69
  1755.6 244.2 %all-reduce.5.cloned.1.call-done = f32[31,1536]{1,0:T(8,128)} async-done(((f32[31,1536]{1,0:T(8,128)}), f32[31,1536]{1,0:T(8,128)}) %all-reduce.5.cloned.1.call-update) | async-done | bytes 190480 | tf_op jit(solution)/shard_map/psum | solution.py:86
  (298 shorter events, 232.0 us)
Async XLA Ops:
  7.2 1645.7 %all-gather.3.cloned.1.call-start = ((), (), s32[]{:S(2)}) async-start(), calls=%async_computation.1 | async-start | bytes 6316032 | tf_op jit(solution)/shard_map/all_gather | solution.py:58
  7.9 1991.8 %all-reduce.5.cloned.1.call-start = ((), (), s32[]{:S(2)}) async-start(), calls=%async_computation | async-start | bytes 393216 | tf_op jit(solution)/shard_map/psum | solution.py:86
  998.0 59.9 %collective-permute-start.66 = (f32[8,1536]{1,0:T(8,128)S(1)}, f32[8,1536]{1,0:T(8,128)S(1)}, u32[]{:S(2)}, u32[]{:S(2)}) collective-permute-start(f32[8,1536]{1,0:T(8,128)S(1)} %fusion), channel_id=1, source_target_pairs={{0,63},{1,64},{2,65},{3,66},{4,67},{5,68},{6,69},{7,70},{8,71},{9,... | collective-permute-start | bytes 147464
  1130.0 56.5 %collective-permute-start.35 = (f32[8,1536]{1,0:T(8,128)S(1)}, f32[8,1536]{1,0:T(8,128)S(1)}, u32[]{:S(2)}, u32[]{:S(2)}) collective-permute-start(f32[8,1536]{1,0:T(8,128)S(1)} %fusion), channel_id=1, source_target_pairs={{0,32},{1,33},{2,34},{3,35},{4,36},{5,37},{6,38},{7,39},{8,40},{9,... | collective-permute-start | bytes 147464
  1132.1 67.6 %collective-permute-start.34 = (f32[8,1536]{1,0:T(8,128)S(1)}, f32[8,1536]{1,0:T(8,128)S(1)}, u32[]{:S(2)}, u32[]{:S(2)}) collective-permute-start(f32[8,1536]{1,0:T(8,128)S(1)} %fusion), channel_id=1, source_target_pairs={{0,31},{1,32},{2,33},{3,34},{4,35},{5,36},{6,37},{7,38},{8,39},{9,... | collective-permute-start | bytes 147464
  1147.1 65.7 %collective-permute-start.33 = (f32[8,1536]{1,0:T(8,128)S(1)}, f32[8,1536]{1,0:T(8,128)S(1)}, u32[]{:S(2)}, u32[]{:S(2)}) collective-permute-start(f32[8,1536]{1,0:T(8,128)S(1)} %fusion), channel_id=1, source_target_pairs={{0,30},{1,31},{2,32},{3,33},{4,34},{5,35},{6,36},{7,37},{8,38},{9,... | collective-permute-start | bytes 147464
  1160.3 65.7 %collective-permute-start.32 = (f32[8,1536]{1,0:T(8,128)S(1)}, f32[8,1536]{1,0:T(8,128)S(1)}, u32[]{:S(2)}, u32[]{:S(2)}) collective-permute-start(f32[8,1536]{1,0:T(8,128)S(1)} %fusion), channel_id=1, source_target_pairs={{0,29},{1,30},{2,31},{3,32},{4,33},{5,34},{6,35},{7,36},{8,37},{9,... | collective-permute-start | bytes 147464
  1173.4 65.7 %collective-permute-start.31 = (f32[8,1536]{1,0:T(8,128)S(1)}, f32[8,1536]{1,0:T(8,128)S(1)}, u32[]{:S(2)}, u32[]{:S(2)}) collective-permute-start(f32[8,1536]{1,0:T(8,128)S(1)} %fusion), channel_id=1, source_target_pairs={{0,28},{1,29},{2,30},{3,31},{4,32},{5,33},{6,34},{7,35},{8,36},{9,... | collective-permute-start | bytes 147464
  1186.6 65.7 %collective-permute-start.30 = (f32[8,1536]{1,0:T(8,128)S(1)}, f32[8,1536]{1,0:T(8,128)S(1)}, u32[]{:S(2)}, u32[]{:S(2)}) collective-permute-start(f32[8,1536]{1,0:T(8,128)S(1)} %fusion), channel_id=1, source_target_pairs={{0,27},{1,28},{2,29},{3,30},{4,31},{5,32},{6,33},{7,34},{8,35},{9,... | collective-permute-start | bytes 147464
  1199.7 65.7 %collective-permute-start.29 = (f32[8,1536]{1,0:T(8,128)S(1)}, f32[8,1536]{1,0:T(8,128)S(1)}, u32[]{:S(2)}, u32[]{:S(2)}) collective-permute-start(f32[8,1536]{1,0:T(8,128)S(1)} %fusion), channel_id=1, source_target_pairs={{0,26},{1,27},{2,28},{3,29},{4,30},{5,31},{6,32},{7,33},{8,34},{9,... | collective-permute-start | bytes 147464
  1212.9 65.7 %collective-permute-start.28 = (f32[8,1536]{1,0:T(8,128)S(1)}, f32[8,1536]{1,0:T(8,128)S(1)}, u32[]{:S(2)}, u32[]{:S(2)}) collective-permute-start(f32[8,1536]{1,0:T(8,128)S(1)} %fusion), channel_id=1, source_target_pairs={{0,25},{1,26},{2,27},{3,28},{4,29},{5,30},{6,31},{7,32},{8,33},{9,... | collective-permute-start | bytes 147464
  1226.0 65.7 %collective-permute-start.27 = (f32[8,1536]{1,0:T(8,128)S(1)}, f32[8,1536]{1,0:T(8,128)S(1)}, u32[]{:S(2)}, u32[]{:S(2)}) collective-permute-start(f32[8,1536]{1,0:T(8,128)S(1)} %fusion), channel_id=1, source_target_pairs={{0,24},{1,25},{2,26},{3,27},{4,28},{5,29},{6,30},{7,31},{8,32},{9,... | collective-permute-start | bytes 147464
  1239.2 65.7 %collective-permute-start.26 = (f32[8,1536]{1,0:T(8,128)S(1)}, f32[8,1536]{1,0:T(8,128)S(1)}, u32[]{:S(2)}, u32[]{:S(2)}) collective-permute-start(f32[8,1536]{1,0:T(8,128)S(1)} %fusion), channel_id=1, source_target_pairs={{0,23},{1,24},{2,25},{3,26},{4,27},{5,28},{6,29},{7,30},{8,31},{9,... | collective-permute-start | bytes 147464
  1252.3 65.7 %collective-permute-start.25 = (f32[8,1536]{1,0:T(8,128)S(1)}, f32[8,1536]{1,0:T(8,128)S(1)}, u32[]{:S(2)}, u32[]{:S(2)}) collective-permute-start(f32[8,1536]{1,0:T(8,128)S(1)} %fusion), channel_id=1, source_target_pairs={{0,22},{1,23},{2,24},{3,25},{4,26},{5,27},{6,28},{7,29},{8,30},{9,... | collective-permute-start | bytes 147464
  1265.5 65.7 %collective-permute-start.24 = (f32[8,1536]{1,0:T(8,128)S(1)}, f32[8,1536]{1,0:T(8,128)S(1)}, u32[]{:S(2)}, u32[]{:S(2)}) collective-permute-start(f32[8,1536]{1,0:T(8,128)S(1)} %fusion), channel_id=1, source_target_pairs={{0,21},{1,22},{2,23},{3,24},{4,25},{5,26},{6,27},{7,28},{8,29},{9,... | collective-permute-start | bytes 147464
  1278.6 65.7 %collective-permute-start.23 = (f32[8,1536]{1,0:T(8,128)S(1)}, f32[8,1536]{1,0:T(8,128)S(1)}, u32[]{:S(2)}, u32[]{:S(2)}) collective-permute-start(f32[8,1536]{1,0:T(8,128)S(1)} %fusion), channel_id=1, source_target_pairs={{0,20},{1,21},{2,22},{3,23},{4,24},{5,25},{6,26},{7,27},{8,28},{9,... | collective-permute-start | bytes 147464
  1291.8 65.7 %collective-permute-start.22 = (f32[8,1536]{1,0:T(8,128)S(1)}, f32[8,1536]{1,0:T(8,128)S(1)}, u32[]{:S(2)}, u32[]{:S(2)}) collective-permute-start(f32[8,1536]{1,0:T(8,128)S(1)} %fusion), channel_id=1, source_target_pairs={{0,19},{1,20},{2,21},{3,22},{4,23},{5,24},{6,25},{7,26},{8,27},{9,... | collective-permute-start | bytes 147464
  1304.9 65.7 %collective-permute-start.21 = (f32[8,1536]{1,0:T(8,128)S(1)}, f32[8,1536]{1,0:T(8,128)S(1)}, u32[]{:S(2)}, u32[]{:S(2)}) collective-permute-start(f32[8,1536]{1,0:T(8,128)S(1)} %fusion), channel_id=1, source_target_pairs={{0,18},{1,19},{2,20},{3,21},{4,22},{5,23},{6,24},{7,25},{8,26},{9,... | collective-permute-start | bytes 147464
  1318.1 65.7 %collective-permute-start.20 = (f32[8,1536]{1,0:T(8,128)S(1)}, f32[8,1536]{1,0:T(8,128)S(1)}, u32[]{:S(2)}, u32[]{:S(2)}) collective-permute-start(f32[8,1536]{1,0:T(8,128)S(1)} %fusion), channel_id=1, source_target_pairs={{0,17},{1,18},{2,19},{3,20},{4,21},{5,22},{6,23},{7,24},{8,25},{9,... | collective-permute-start | bytes 147464
  1331.2 65.7 %collective-permute-start.19 = (f32[8,1536]{1,0:T(8,128)S(1)}, f32[8,1536]{1,0:T(8,128)S(1)}, u32[]{:S(2)}, u32[]{:S(2)}) collective-permute-start(f32[8,1536]{1,0:T(8,128)S(1)} %fusion), channel_id=1, source_target_pairs={{0,16},{1,17},{2,18},{3,19},{4,20},{5,21},{6,22},{7,23},{8,24},{9,... | collective-permute-start | bytes 147464
  1344.4 65.7 %collective-permute-start.18 = (f32[8,1536]{1,0:T(8,128)S(1)}, f32[8,1536]{1,0:T(8,128)S(1)}, u32[]{:S(2)}, u32[]{:S(2)}) collective-permute-start(f32[8,1536]{1,0:T(8,128)S(1)} %fusion), channel_id=1, source_target_pairs={{0,15},{1,16},{2,17},{3,18},{4,19},{5,20},{6,21},{7,22},{8,23},{9,... | collective-permute-start | bytes 147464
  1357.5 65.7 %collective-permute-start.17 = (f32[8,1536]{1,0:T(8,128)S(1)}, f32[8,1536]{1,0:T(8,128)S(1)}, u32[]{:S(2)}, u32[]{:S(2)}) collective-permute-start(f32[8,1536]{1,0:T(8,128)S(1)} %fusion), channel_id=1, source_target_pairs={{0,14},{1,15},{2,16},{3,17},{4,18},{5,19},{6,20},{7,21},{8,22},{9,... | collective-permute-start | bytes 147464
  1370.7 65.7 %collective-permute-start.16 = (f32[8,1536]{1,0:T(8,128)S(1)}, f32[8,1536]{1,0:T(8,128)S(1)}, u32[]{:S(2)}, u32[]{:S(2)}) collective-permute-start(f32[8,1536]{1,0:T(8,128)S(1)} %fusion), channel_id=1, source_target_pairs={{0,13},{1,14},{2,15},{3,16},{4,17},{5,18},{6,19},{7,20},{8,21},{9,... | collective-permute-start | bytes 147464
  1383.8 65.7 %collective-permute-start.15 = (f32[8,1536]{1,0:T(8,128)S(1)}, f32[8,1536]{1,0:T(8,128)S(1)}, u32[]{:S(2)}, u32[]{:S(2)}) collective-permute-start(f32[8,1536]{1,0:T(8,128)S(1)} %fusion), channel_id=1, source_target_pairs={{0,12},{1,13},{2,14},{3,15},{4,16},{5,17},{6,18},{7,19},{8,20},{9,... | collective-permute-start | bytes 147464
  1397.0 65.7 %collective-permute-start.14 = (f32[8,1536]{1,0:T(8,128)S(1)}, f32[8,1536]{1,0:T(8,128)S(1)}, u32[]{:S(2)}, u32[]{:S(2)}) collective-permute-start(f32[8,1536]{1,0:T(8,128)S(1)} %fusion), channel_id=1, source_target_pairs={{0,11},{1,12},{2,13},{3,14},{4,15},{5,16},{6,17},{7,18},{8,19},{9,... | collective-permute-start | bytes 147464
  1410.1 65.7 %collective-permute-start.13 = (f32[8,1536]{1,0:T(8,128)S(1)}, f32[8,1536]{1,0:T(8,128)S(1)}, u32[]{:S(2)}, u32[]{:S(2)}) collective-permute-start(f32[8,1536]{1,0:T(8,128)S(1)} %fusion), channel_id=1, source_target_pairs={{0,10},{1,11},{2,12},{3,13},{4,14},{5,15},{6,16},{7,17},{8,18},{9,... | collective-permute-start | bytes 147464
  1423.3 65.7 %collective-permute-start.12 = (f32[8,1536]{1,0:T(8,128)S(1)}, f32[8,1536]{1,0:T(8,128)S(1)}, u32[]{:S(2)}, u32[]{:S(2)}) collective-permute-start(f32[8,1536]{1,0:T(8,128)S(1)} %fusion), channel_id=1, source_target_pairs={{0,9},{1,10},{2,11},{3,12},{4,13},{5,14},{6,15},{7,16},{8,17},{9,1... | collective-permute-start | bytes 147464
  1436.4 65.7 %collective-permute-start.11 = (f32[8,1536]{1,0:T(8,128)S(1)}, f32[8,1536]{1,0:T(8,128)S(1)}, u32[]{:S(2)}, u32[]{:S(2)}) collective-permute-start(f32[8,1536]{1,0:T(8,128)S(1)} %fusion), channel_id=1, source_target_pairs={{0,8},{1,9},{2,10},{3,11},{4,12},{5,13},{6,14},{7,15},{8,16},{9,17... | collective-permute-start | bytes 147464
  1449.6 65.7 %collective-permute-start.10 = (f32[8,1536]{1,0:T(8,128)S(1)}, f32[8,1536]{1,0:T(8,128)S(1)}, u32[]{:S(2)}, u32[]{:S(2)}) collective-permute-start(f32[8,1536]{1,0:T(8,128)S(1)} %fusion), channel_id=1, source_target_pairs={{0,7},{1,8},{2,9},{3,10},{4,11},{5,12},{6,13},{7,14},{8,15},{9,16}... | collective-permute-start | bytes 147464
  1462.7 65.7 %collective-permute-start.9 = (f32[8,1536]{1,0:T(8,128)S(1)}, f32[8,1536]{1,0:T(8,128)S(1)}, u32[]{:S(2)}, u32[]{:S(2)}) collective-permute-start(f32[8,1536]{1,0:T(8,128)S(1)} %fusion), channel_id=1, source_target_pairs={{0,6},{1,7},{2,8},{3,9},{4,10},{5,11},{6,12},{7,13},{8,14},{9,15},... | collective-permute-start | bytes 147464
  1475.9 66.3 %collective-permute-start.8 = (f32[8,1536]{1,0:T(8,128)S(1)}, f32[8,1536]{1,0:T(8,128)}, u32[]{:S(2)}, u32[]{:S(2)}) collective-permute-start(f32[8,1536]{1,0:T(8,128)S(1)} %fusion), channel_id=1, source_target_pairs={{0,5},{1,6},{2,7},{3,8},{4,9},{5,10},{6,11},{7,12},{8,13},{9,14},{... | collective-permute-start | bytes 147464
  1489.0 53.1 %collective-permute-start.7 = (f32[8,1536]{1,0:T(8,128)S(1)}, f32[8,1536]{1,0:T(8,128)}, u32[]{:S(2)}, u32[]{:S(2)}) collective-permute-start(f32[8,1536]{1,0:T(8,128)S(1)} %fusion), channel_id=1, source_target_pairs={{0,4},{1,5},{2,6},{3,7},{4,8},{5,9},{6,10},{7,11},{8,12},{9,13},{1... | collective-permute-start | bytes 147464
  (101 other events, 10017.7 us)
Sparse Core Ops, SparseCore 0:
  9.9 738.2 all-gather.2
  1751.2 248.4 all-reduce.4
where the time goes:
time: 2010 us
  blocking collectives  1040 us (52%)
  starting transfers between devices  550 us (27%)
  waiting for transfers between devices  259 us (13%)
  local copies, waits for them, and re-layouts  115 us (6%)
    unnamed x1, blocking collectives  808 us
    unnamed x64, starting transfers between devices  541 us
    psum x1, waiting for transfers between devices, on_device(): kernel_grad = lax.psum(jnp.stack(tap_rows), ('dp', 'seq'))  244 us
    unnamed x130, local copies, waits for them, and re-layouts  108 us
    psum x1, blocking collectives, on_device(): lax.psum(jnp.sum(jnp.where(valid, conv_out, 0.0), axis=0), ('dp', 'seq'))  85.3 us
    psum x1, blocking collectives, on_device(): spread = lax.psum(jnp.sum(deviation * deviation, axis=0), ('dp', 'seq'))  73.7 us
    psum x1, blocking collectives, on_device(): lax.psum((jnp.sum(scaled_grad * standard, axis=0), jnp.sum(scaled_grad, a...  72.6 us
  transfers between devices with their start and end apart: 70, of which 3 were waited for; matrix products, arithmetic and copies ran while one was open for 46% of the time, Pallas kernels for 0%

commit v1 on v0

--- a/solution.py
+++ b/solution.py
@@ -41,7 +41,9 @@
     conv_out = jnp.zeros((frames, masked.shape[1]), jnp.float32)
     for tap in range(KERNEL):
         conv_out = conv_out + kernel[tap] * padded[tap : tap + frames]
-    total = lax.psum(jnp.sum(jnp.where(valid, conv_out, 0.0), axis=0), ("dp", "seq"))
+    total = jnp.sum(
+        lax.all_gather(jnp.sum(jnp.where(valid, conv_out, 0.0), axis=0), ("dp", "seq")), axis=0
+    )
     channel_mean = total / count
     deviation = jnp.where(valid, conv_out - channel_mean, 0.0)
     spread = lax.psum(jnp.sum(deviation * deviation, axis=0), ("dp", "seq"))

time: 2010 us -> 2630 us (1.31)
  waiting for transfers between devices: 259 us -> 954 us
  blocking collectives: 1040 us -> 954 us
    all_gather x0 -> x1, waiting for transfers between devices: none -> 695 us  [on_device(): lax.all_gather(jnp.sum(jnp.where(valid, conv_out, 0.0), axis=0), ('dp', '...]
    psum x1 -> x0, blocking collectives: 85.3 us -> none  [on_device(): lax.psum(jnp.sum(jnp.where(valid, conv_out, 0.0), axis=0), ('dp', 'seq'))]
    unnamed x130 -> x133, local copies, waits for them, and re-layouts: 108 us -> 109 us
  transfers between devices with their start and end apart: 70 -> 71, of which waited for: 3 -> 4; matrix products, arithmetic and copies ran while one was open for 46% -> 35% of each run, Pallas kernels for 0% -> 0%
where the time goes in v1:
time: 2630 us; the launch traced here: 2620 us
  waiting for transfers between devices  954 us (36%)
  blocking collectives  954 us (36%)
  starting transfers between devices  551 us (21%)
  local copies, waits for them, and re-layouts  116 us (4%)
    unnamed x1, blocking collectives  803 us
    all_gather x1, waiting for transfers between devices, on_device(): lax.all_gather(jnp.sum(jnp.where(valid, conv_out, 0.0), axis=0), ('dp', '...  695 us
    unnamed x64, starting transfers between devices  541 us
    psum x1, waiting for transfers between devices, on_device(): kernel_grad = lax.psum(jnp.stack(tap_rows), ('dp', 'seq'))  244 us
    unnamed x133, local copies, waits for them, and re-layouts  109 us
    psum x1, blocking collectives, on_device(): spread = lax.psum(jnp.sum(deviation * deviation, axis=0), ('dp', 'seq'))  78.4 us
    psum x1, blocking collectives, on_device(): lax.psum((jnp.sum(scaled_grad * standard, axis=0), jnp.sum(scaled_grad, a...  72.6 us
  transfers between devices with their start and end apart: 71, of which 4 were waited for; matrix products, arithmetic and copies ran while one was open for 35% of the time, Pallas kernels for 0%

profile of v1, /device:TPU:1, one launch (start us, length us, event | category | flops | bytes accessed | tf_op | source)
XLA Modules:
  0.0 2620.8 jit_solution(12372029673637899977)
XLA Ops:
  25.6 694.7 %all-gather.6.cloned.1.call-done = f32[256,1,1536]{2,1,0:T(1,128)} async-done(((f32[1,1,1536]{2,1,0:T(1,128)}), f32[256,1,1536]{2,1,0:T(1,128)}) %all-gather.6.cloned.1.call-update) | async-done | bytes 1572880 | tf_op jit(solution)/shard_map/all_gather | solution.py:45
  722.9 78.4 %psum.28 = f32[1536]{0:T(1024)S(1)} all-reduce(f32[1536]{0:T(1024)S(1)} %multiply_reduce_fusion.32), channel_id=1, replica_groups=mesh['dp'=4,'seq'=64] {'dp','seq'}, use_global_device_ids=true, to_apply=%region_4.5 | all-reduce | flops 1536 | bytes 12288 | tf_op jit(solution)/shard_map/psum | solution.py:49
  806.5 803.2 %fusion = f32[8,1536]{1,0:T(8,128)S(1)} fusion(f32[1536,1536]{1,0:T(8,128)} %fusion.95), kind=kCustom, calls=%all-reduce-scatter | all-reduce-scatter fusion | flops 3145729 | bytes 9486336
  1609.7 48.5 %collective-permute-start.66 = (f32[8,1536]{1,0:T(8,128)S(1)}, f32[8,1536]{1,0:T(8,128)S(1)}, u32[]{:S(2)}, u32[]{:S(2)}) collective-permute-start(f32[8,1536]{1,0:T(8,128)S(1)} %fusion), channel_id=1, source_target_pairs={{0,63},{1,64},{2,65},{3,66},{4,67},{5,68},{6,69},{7,70},{8,71},{9,... | collective-permute-start | bytes 147464
  1759.9 13.1 collective-permute-start.33
  1773.0 13.1 collective-permute-start.32
  1786.2 13.1 collective-permute-start.31
  1799.3 13.1 collective-permute-start.30
  1812.5 13.1 collective-permute-start.29
  1825.6 13.1 collective-permute-start.28
  1838.8 13.1 collective-permute-start.27
  1851.9 13.1 collective-permute-start.26
  1865.1 13.1 collective-permute-start.25
  1878.2 13.1 collective-permute-start.24
  1891.4 13.1 collective-permute-start.23
  1904.5 13.1 collective-permute-start.22
  1917.7 13.1 collective-permute-start.21
  1930.8 13.1 collective-permute-start.20
  1944.0 13.1 collective-permute-start.19
  1957.1 13.1 collective-permute-start.18
  1970.3 13.1 collective-permute-start.17
  1983.4 13.1 collective-permute-start.16
  1996.6 13.1 collective-permute-start.15
  2009.7 13.1 collective-permute-start.14
  2088.6 13.1 collective-permute-start.8
  2101.8 13.1 collective-permute-start.7
  2114.9 13.1 collective-permute-start.6
  2128.1 13.1 collective-permute-start.5
  2141.2 13.3 collective-permute-start.4
  2166.9 97.0 %concatenate.41 = f32[518,1536]{1,0:T(8,128)} concatenate(f32[6,1536]{1,0:T(8,128)S(1)} %collective-permute-done.67, f32[8,1536]{1,0:T(8,128)S(1)} %collective-permute-done.66, f32[8,1536]{1,0:T(8,128)S(1)} %collective-permute-done.65, f32[8,1536]{1,0:T(8,128)S(1)} %collective-permute-done.64, f32[8,1536]{1,0:T(8,128)S(1)} %collective-permute-done.63, ...), dimensions={0} | concatenate | bytes 6365184
  2278.1 72.6 %all-reduce.2 = (f32[1536]{0:T(1024)}, f32[1536]{0:T(1024)S(1)}) all-reduce(f32[1536]{0:T(1024)S(1)} %get-tuple-element.40, f32[1536]{0:T(1024)S(1)} %get-tuple-element.39), channel_id=1, replica_groups=mesh['dp'=4,'seq'=64] {'dp','seq'}, use_global_device_ids=true, to_apply=%region_8.9 | all-reduce | flops 3072 | bytes 24576 | tf_op jit(solution)/shard_map/psum | solution.py:71
  2368.3 244.3 %all-reduce.5.cloned.1.call-done = f32[31,1536]{1,0:T(8,128)} async-done(((f32[31,1536]{1,0:T(8,128)}), f32[31,1536]{1,0:T(8,128)}) %all-reduce.5.cloned.1.call-update) | async-done | bytes 190480 | tf_op jit(solution)/shard_map/psum | solution.py:88
  (304 shorter events, 237.0 us)
Async XLA Ops:
  7.2 713.2 %all-gather.6.cloned.1.call-start = ((), (), s32[]{:S(2)}) async-start(), calls=%async_computation.1 | async-start | bytes 1579008 | tf_op jit(solution)/shard_map/all_gather | solution.py:45
  23.5 2242.0 %all-gather.8.cloned.1.call-start = ((), (), s32[]{:S(2)}) async-start(), calls=%async_computation.2 | async-start | bytes 6316032 | tf_op jit(solution)/shard_map/all_gather | solution.py:60
  24.3 2588.3 %all-reduce.5.cloned.1.call-start = ((), (), s32[]{:S(2)}) async-start(), calls=%async_computation | async-start | bytes 393216 | tf_op jit(solution)/shard_map/psum | solution.py:88
  1609.7 60.2 %collective-permute-start.66 = (f32[8,1536]{1,0:T(8,128)S(1)}, f32[8,1536]{1,0:T(8,128)S(1)}, u32[]{:S(2)}, u32[]{:S(2)}) collective-permute-start(f32[8,1536]{1,0:T(8,128)S(1)} %fusion), channel_id=1, source_target_pairs={{0,63},{1,64},{2,65},{3,66},{4,67},{5,68},{6,69},{7,70},{8,71},{9,... | collective-permute-start | bytes 147464
  1748.3 64.2 %collective-permute-start.34 = (f32[8,1536]{1,0:T(8,128)S(1)}, f32[8,1536]{1,0:T(8,128)S(1)}, u32[]{:S(2)}, u32[]{:S(2)}) collective-permute-start(f32[8,1536]{1,0:T(8,128)S(1)} %fusion), channel_id=1, source_target_pairs={{0,31},{1,32},{2,33},{3,34},{4,35},{5,36},{6,37},{7,38},{8,39},{9,... | collective-permute-start | bytes 147464
  1759.9 65.7 %collective-permute-start.33 = (f32[8,1536]{1,0:T(8,128)S(1)}, f32[8,1536]{1,0:T(8,128)S(1)}, u32[]{:S(2)}, u32[]{:S(2)}) collective-permute-start(f32[8,1536]{1,0:T(8,128)S(1)} %fusion), channel_id=1, source_target_pairs={{0,30},{1,31},{2,32},{3,33},{4,34},{5,35},{6,36},{7,37},{8,38},{9,... | collective-permute-start | bytes 147464
  1773.0 65.7 %collective-permute-start.32 = (f32[8,1536]{1,0:T(8,128)S(1)}, f32[8,1536]{1,0:T(8,128)S(1)}, u32[]{:S(2)}, u32[]{:S(2)}) collective-permute-start(f32[8,1536]{1,0:T(8,128)S(1)} %fusion), channel_id=1, source_target_pairs={{0,29},{1,30},{2,31},{3,32},{4,33},{5,34},{6,35},{7,36},{8,37},{9,... | collective-permute-start | bytes 147464
  1786.2 65.7 %collective-permute-start.31 = (f32[8,1536]{1,0:T(8,128)S(1)}, f32[8,1536]{1,0:T(8,128)S(1)}, u32[]{:S(2)}, u32[]{:S(2)}) collective-permute-start(f32[8,1536]{1,0:T(8,128)S(1)} %fusion), channel_id=1, source_target_pairs={{0,28},{1,29},{2,30},{3,31},{4,32},{5,33},{6,34},{7,35},{8,36},{9,... | collective-permute-start | bytes 147464
  1799.3 65.7 %collective-permute-start.30 = (f32[8,1536]{1,0:T(8,128)S(1)}, f32[8,1536]{1,0:T(8,128)S(1)}, u32[]{:S(2)}, u32[]{:S(2)}) collective-permute-start(f32[8,1536]{1,0:T(8,128)S(1)} %fusion), channel_id=1, source_target_pairs={{0,27},{1,28},{2,29},{3,30},{4,31},{5,32},{6,33},{7,34},{8,35},{9,... | collective-permute-start | bytes 147464
  1812.5 65.7 %collective-permute-start.29 = (f32[8,1536]{1,0:T(8,128)S(1)}, f32[8,1536]{1,0:T(8,128)S(1)}, u32[]{:S(2)}, u32[]{:S(2)}) collective-permute-start(f32[8,1536]{1,0:T(8,128)S(1)} %fusion), channel_id=1, source_target_pairs={{0,26},{1,27},{2,28},{3,29},{4,30},{5,31},{6,32},{7,33},{8,34},{9,... | collective-permute-start | bytes 147464
  1825.6 65.7 %collective-permute-start.28 = (f32[8,1536]{1,0:T(8,128)S(1)}, f32[8,1536]{1,0:T(8,128)S(1)}, u32[]{:S(2)}, u32[]{:S(2)}) collective-permute-start(f32[8,1536]{1,0:T(8,128)S(1)} %fusion), channel_id=1, source_target_pairs={{0,25},{1,26},{2,27},{3,28},{4,29},{5,30},{6,31},{7,32},{8,33},{9,... | collective-permute-start | bytes 147464
  1838.8 65.7 %collective-permute-start.27 = (f32[8,1536]{1,0:T(8,128)S(1)}, f32[8,1536]{1,0:T(8,128)S(1)}, u32[]{:S(2)}, u32[]{:S(2)}) collective-permute-start(f32[8,1536]{1,0:T(8,128)S(1)} %fusion), channel_id=1, source_target_pairs={{0,24},{1,25},{2,26},{3,27},{4,28},{5,29},{6,30},{7,31},{8,32},{9,... | collective-permute-start | bytes 147464
  1851.9 65.7 %collective-permute-start.26 = (f32[8,1536]{1,0:T(8,128)S(1)}, f32[8,1536]{1,0:T(8,128)S(1)}, u32[]{:S(2)}, u32[]{:S(2)}) collective-permute-start(f32[8,1536]{1,0:T(8,128)S(1)} %fusion), channel_id=1, source_target_pairs={{0,23},{1,24},{2,25},{3,26},{4,27},{5,28},{6,29},{7,30},{8,31},{9,... | collective-permute-start | bytes 147464
  1865.1 65.7 %collective-permute-start.25 = (f32[8,1536]{1,0:T(8,128)S(1)}, f32[8,1536]{1,0:T(8,128)S(1)}, u32[]{:S(2)}, u32[]{:S(2)}) collective-permute-start(f32[8,1536]{1,0:T(8,128)S(1)} %fusion), channel_id=1, source_target_pairs={{0,22},{1,23},{2,24},{3,25},{4,26},{5,27},{6,28},{7,29},{8,30},{9,... | collective-permute-start | bytes 147464
  1878.2 65.7 %collective-permute-start.24 = (f32[8,1536]{1,0:T(8,128)S(1)}, f32[8,1536]{1,0:T(8,128)S(1)}, u32[]{:S(2)}, u32[]{:S(2)}) collective-permute-start(f32[8,1536]{1,0:T(8,128)S(1)} %fusion), channel_id=1, source_target_pairs={{0,21},{1,22},{2,23},{3,24},{4,25},{5,26},{6,27},{7,28},{8,29},{9,... | collective-permute-start | bytes 147464
  1891.4 65.7 %collective-permute-start.23 = (f32[8,1536]{1,0:T(8,128)S(1)}, f32[8,1536]{1,0:T(8,128)S(1)}, u32[]{:S(2)}, u32[]{:S(2)}) collective-permute-start(f32[8,1536]{1,0:T(8,128)S(1)} %fusion), channel_id=1, source_target_pairs={{0,20},{1,21},{2,22},{3,23},{4,24},{5,25},{6,26},{7,27},{8,28},{9,... | collective-permute-start | bytes 147464
  1904.5 65.7 %collective-permute-start.22 = (f32[8,1536]{1,0:T(8,128)S(1)}, f32[8,1536]{1,0:T(8,128)S(1)}, u32[]{:S(2)}, u32[]{:S(2)}) collective-permute-start(f32[8,1536]{1,0:T(8,128)S(1)} %fusion), channel_id=1, source_target_pairs={{0,19},{1,20},{2,21},{3,22},{4,23},{5,24},{6,25},{7,26},{8,27},{9,... | collective-permute-start | bytes 147464
  1917.7 65.7 %collective-permute-start.21 = (f32[8,1536]{1,0:T(8,128)S(1)}, f32[8,1536]{1,0:T(8,128)S(1)}, u32[]{:S(2)}, u32[]{:S(2)}) collective-permute-start(f32[8,1536]{1,0:T(8,128)S(1)} %fusion), channel_id=1, source_target_pairs={{0,18},{1,19},{2,20},{3,21},{4,22},{5,23},{6,24},{7,25},{8,26},{9,... | collective-permute-start | bytes 147464
  1930.8 65.7 %collective-permute-start.20 = (f32[8,1536]{1,0:T(8,128)S(1)}, f32[8,1536]{1,0:T(8,128)S(1)}, u32[]{:S(2)}, u32[]{:S(2)}) collective-permute-start(f32[8,1536]{1,0:T(8,128)S(1)} %fusion), channel_id=1, source_target_pairs={{0,17},{1,18},{2,19},{3,20},{4,21},{5,22},{6,23},{7,24},{8,25},{9,... | collective-permute-start | bytes 147464
  1944.0 65.7 %collective-permute-start.19 = (f32[8,1536]{1,0:T(8,128)S(1)}, f32[8,1536]{1,0:T(8,128)S(1)}, u32[]{:S(2)}, u32[]{:S(2)}) collective-permute-start(f32[8,1536]{1,0:T(8,128)S(1)} %fusion), channel_id=1, source_target_pairs={{0,16},{1,17},{2,18},{3,19},{4,20},{5,21},{6,22},{7,23},{8,24},{9,... | collective-permute-start | bytes 147464
  1957.1 65.7 %collective-permute-start.18 = (f32[8,1536]{1,0:T(8,128)S(1)}, f32[8,1536]{1,0:T(8,128)S(1)}, u32[]{:S(2)}, u32[]{:S(2)}) collective-permute-start(f32[8,1536]{1,0:T(8,128)S(1)} %fusion), channel_id=1, source_target_pairs={{0,15},{1,16},{2,17},{3,18},{4,19},{5,20},{6,21},{7,22},{8,23},{9,... | collective-permute-start | bytes 147464
  1970.3 65.7 %collective-permute-start.17 = (f32[8,1536]{1,0:T(8,128)S(1)}, f32[8,1536]{1,0:T(8,128)S(1)}, u32[]{:S(2)}, u32[]{:S(2)}) collective-permute-start(f32[8,1536]{1,0:T(8,128)S(1)} %fusion), channel_id=1, source_target_pairs={{0,14},{1,15},{2,16},{3,17},{4,18},{5,19},{6,20},{7,21},{8,22},{9,... | collective-permute-start | bytes 147464
  1983.4 65.7 %collective-permute-start.16 = (f32[8,1536]{1,0:T(8,128)S(1)}, f32[8,1536]{1,0:T(8,128)S(1)}, u32[]{:S(2)}, u32[]{:S(2)}) collective-permute-start(f32[8,1536]{1,0:T(8,128)S(1)} %fusion), channel_id=1, source_target_pairs={{0,13},{1,14},{2,15},{3,16},{4,17},{5,18},{6,19},{7,20},{8,21},{9,... | collective-permute-start | bytes 147464
  1996.6 65.7 %collective-permute-start.15 = (f32[8,1536]{1,0:T(8,128)S(1)}, f32[8,1536]{1,0:T(8,128)S(1)}, u32[]{:S(2)}, u32[]{:S(2)}) collective-permute-start(f32[8,1536]{1,0:T(8,128)S(1)} %fusion), channel_id=1, source_target_pairs={{0,12},{1,13},{2,14},{3,15},{4,16},{5,17},{6,18},{7,19},{8,20},{9,... | collective-permute-start | bytes 147464
  2009.7 65.7 %collective-permute-start.14 = (f32[8,1536]{1,0:T(8,128)S(1)}, f32[8,1536]{1,0:T(8,128)S(1)}, u32[]{:S(2)}, u32[]{:S(2)}) collective-permute-start(f32[8,1536]{1,0:T(8,128)S(1)} %fusion), channel_id=1, source_target_pairs={{0,11},{1,12},{2,13},{3,14},{4,15},{5,16},{6,17},{7,18},{8,19},{9,... | collective-permute-start | bytes 147464
  2022.9 65.7 %collective-permute-start.13 = (f32[8,1536]{1,0:T(8,128)S(1)}, f32[8,1536]{1,0:T(8,128)S(1)}, u32[]{:S(2)}, u32[]{:S(2)}) collective-permute-start(f32[8,1536]{1,0:T(8,128)S(1)} %fusion), channel_id=1, source_target_pairs={{0,10},{1,11},{2,12},{3,13},{4,14},{5,15},{6,16},{7,17},{8,18},{9,... | collective-permute-start | bytes 147464
  2036.0 65.7 %collective-permute-start.12 = (f32[8,1536]{1,0:T(8,128)S(1)}, f32[8,1536]{1,0:T(8,128)S(1)}, u32[]{:S(2)}, u32[]{:S(2)}) collective-permute-start(f32[8,1536]{1,0:T(8,128)S(1)} %fusion), channel_id=1, source_target_pairs={{0,9},{1,10},{2,11},{3,12},{4,13},{5,14},{6,15},{7,16},{8,17},{9,1... | collective-permute-start | bytes 147464
  2049.2 65.7 %collective-permute-start.11 = (f32[8,1536]{1,0:T(8,128)S(1)}, f32[8,1536]{1,0:T(8,128)S(1)}, u32[]{:S(2)}, u32[]{:S(2)}) collective-permute-start(f32[8,1536]{1,0:T(8,128)S(1)} %fusion), channel_id=1, source_target_pairs={{0,8},{1,9},{2,10},{3,11},{4,12},{5,13},{6,14},{7,15},{8,16},{9,17... | collective-permute-start | bytes 147464
  2062.3 65.7 %collective-permute-start.10 = (f32[8,1536]{1,0:T(8,128)S(1)}, f32[8,1536]{1,0:T(8,128)S(1)}, u32[]{:S(2)}, u32[]{:S(2)}) collective-permute-start(f32[8,1536]{1,0:T(8,128)S(1)} %fusion), channel_id=1, source_target_pairs={{0,7},{1,8},{2,9},{3,10},{4,11},{5,12},{6,13},{7,14},{8,15},{9,16}... | collective-permute-start | bytes 147464
  2075.5 65.7 %collective-permute-start.9 = (f32[8,1536]{1,0:T(8,128)S(1)}, f32[8,1536]{1,0:T(8,128)S(1)}, u32[]{:S(2)}, u32[]{:S(2)}) collective-permute-start(f32[8,1536]{1,0:T(8,128)S(1)} %fusion), channel_id=1, source_target_pairs={{0,6},{1,7},{2,8},{3,9},{4,10},{5,11},{6,12},{7,13},{8,14},{9,15},... | collective-permute-start | bytes 147464
  2088.6 66.3 %collective-permute-start.8 = (f32[8,1536]{1,0:T(8,128)S(1)}, f32[8,1536]{1,0:T(8,128)}, u32[]{:S(2)}, u32[]{:S(2)}) collective-permute-start(f32[8,1536]{1,0:T(8,128)S(1)} %fusion), channel_id=1, source_target_pairs={{0,5},{1,6},{2,7},{3,8},{4,9},{5,10},{6,11},{7,12},{8,13},{9,14},{... | collective-permute-start | bytes 147464
  2101.8 53.1 %collective-permute-start.7 = (f32[8,1536]{1,0:T(8,128)S(1)}, f32[8,1536]{1,0:T(8,128)}, u32[]{:S(2)}, u32[]{:S(2)}) collective-permute-start(f32[8,1536]{1,0:T(8,128)S(1)} %fusion), channel_id=1, source_target_pairs={{0,4},{1,5},{2,6},{3,7},{4,8},{5,9},{6,10},{7,11},{8,12},{9,13},{1... | collective-permute-start | bytes 147464
  (103 other events, 12518.9 us)
Sparse Core Ops, SparseCore 0:
  23.7 696.6 all-gather.5
  722.2 728.3 all-gather.7
  2363.9 248.6 all-reduce.4
